TPU v7x, 32 devices: a whole 2x2x4 slice. The times are simulated.
32 devices in a mesh: groups: 2 (over y), occ: 4 (over z), vir: 4 (over x, core).
Axes of the slice: x: 2, y: 2, z: 4, core: 2. Of those that a mesh axis runs over, the one named last changes fastest.
Arguments:
- amplitudes: bfloat16 [32, 400, 24, 128], P(('groups', 'occ'), None, 'vir'), parts along dimension 0, may hold values from -6 to 6
- amp_keep: int32 [32, 24], P(('groups', 'occ'), 'vir'), parts along dimension 0, may hold values 0 or 1
- integrals: bfloat16 [48, 128, 24, 128], P(('groups', 'vir')), parts along dimension 0, may hold values from -0.3125 to 0.3125
- int_keep: int32 [48, 24], P(('groups', 'vir')), parts along dimension 0, may hold values 0 or 1
- fock_vir: bfloat16 [48, 128, 128], P(('groups', 'vir')), parts along dimension 0, may hold values from -0.5 to 0.5
- fock_occ: bfloat16 [32, 400, 400], P(('groups', 'occ')), parts along dimension 0, may hold values from -0.3125 to 0.3125
- occ_energy: float32 [32, 400], P(('groups', 'occ')), parts along dimension 0, may hold values from -2 to -0.4
- vir_energy: float32 [48, 128], P(('groups', 'vir')), parts along dimension 0, may hold values from 0.4 to 3
- res_keep: int32 [32, 24], P(('groups', 'occ'), 'vir'), parts along dimension 0, may hold values 0 or 1
- res_place: int32 [32, 24], P(('groups', 'occ'), 'vir'), parts along dimension 0, may hold values from 0 to 95, as said below
Outputs:
- residual_tiles: float32 [192, 4, 400, 128], P(('groups', 'occ'), 'vir'), parts along dimension 0
- new_amplitudes: float32 [192, 4, 400, 128], P(('groups', 'occ'), 'vir'), parts along dimension 0
There are 2 independent parts, one for each index of `groups`. A program takes and returns all parts, laid end to end along the dimension named above; each array names one. Nothing has to cross between parts.
Inputs may be any that keep to these rules, and one draw needn't show every extreme that they name: Within each run of 6 virtual tiles, res_place maps the tiles of all pair tiles one to one onto 0 to 95. The tiles of one aligned run of 4 pair tiles within one such virtual run reach at most 6 values in any aligned run of 24 values, and exactly 6 in some.
All inputs are finite; a program needn't handle non-finite values. No bound on the sum of `amp_keep` or of `int_keep` or of `res_keep` on one device may be relied on, other than what follows from the above.
Results may differ from a plain program's by a relative error of at most 0.0003.
Values may be sent and summed in bfloat16 or wider, within the bound.
No kernel may reach another device: no remote copies, remote signals or barrier semaphores. Data moves between devices by JAX's collectives and lax.ppermute only.
A program may use at most 128 MiB of HBM per device.

v0:
```python
import jax
import jax.numpy as jnp
from jax import lax
from jax.sharding import PartitionSpec as P


def body(
    amplitudes,
    amp_keep,
    integrals,
    int_keep,
    fock_vir,
    fock_occ,
    occ_energy,
    vir_energy,
    res_keep,
    res_place,
):
    pair_count, row_count, block_count, tile_width = amplitudes.shape
    sources = lax.axis_size("occ")
    tiles_dev = pair_count * block_count
    capacity = max(2, (tiles_dev + sources - 1) // sources)
    kept_amps = amplitudes * amp_keep[:, None, :, None].astype(jnp.bfloat16)
    masked_ints = integrals * int_keep[:, None, :, None].astype(jnp.bfloat16)
    flat_amps = kept_amps.reshape(pair_count * row_count, block_count, tile_width)
    ladder = lax.psum_scatter(
        jnp.einsum("rkc,kcAa->Ara", flat_amps, masked_ints, preferred_element_type=jnp.float32),
        "vir",
        scatter_dimension=0,
        tiled=True,
    )
    ladder = ladder.reshape(block_count, pair_count, row_count, tile_width)
    vir_term = jnp.einsum("prAc,Aca->Apra", kept_amps, fock_vir, preferred_element_type=jnp.float32)
    occ_term = jnp.einsum("prs,psAa->Apra", fock_occ, kept_amps, preferred_element_type=jnp.float32)
    keep_mask = jnp.transpose(res_keep).astype(jnp.float32)[:, :, None, None]
    resid = keep_mask * (ladder + vir_term - occ_term)
    amps_moved = jnp.transpose(kept_amps, (2, 0, 1, 3))
    res_flat = resid.reshape(tiles_dev, row_count, tile_width)
    places = jnp.transpose(res_place).reshape(tiles_dev)
    target = places // tiles_dev
    own_slot = places % tiles_dev
    order = jnp.arange(tiles_dev, dtype=jnp.int32)
    earlier = (target[None, :] == target[:, None]) & (order[None, :] < order[:, None])
    rank = jnp.sum(earlier.astype(jnp.int32), axis=1)
    match = (target[None, None, :] == jnp.arange(sources, dtype=jnp.int32)[:, None, None]) & (
        rank[None, None, :] == jnp.arange(capacity, dtype=jnp.int32)[None, :, None]
    )
    chosen = jnp.sum(jnp.where(match, order[None, None, :], 0), axis=2)
    filled = jnp.any(match, axis=2)
    send_res = jnp.where(filled[:, :, None, None], res_flat[chosen], 0.0)
    every_row = jnp.arange(sources * capacity, dtype=jnp.int32)
    denominator = vir_energy[:, None, None, :] - occ_energy[None, :, :, None]
    update = amps_moved.astype(jnp.float32) + resid / denominator
    upd_flat = update.reshape(tiles_dev, row_count, tile_width)
    send_upd = jnp.where(filled[:, :, None, None], upd_flat[chosen], 0.0)
    send_slot = jnp.where(filled, own_slot[chosen], -1)
    got_res, got_upd, got_slot = (
        lax.all_to_all(send_res, "occ", split_axis=0, concat_axis=0, tiled=True),
        lax.all_to_all(send_upd, "occ", split_axis=0, concat_axis=0, tiled=True),
        lax.all_to_all(send_slot, "occ", split_axis=0, concat_axis=0, tiled=True),
    )
    got_res = got_res.reshape(sources * capacity, row_count, tile_width)
    got_upd = got_upd.reshape(sources * capacity, row_count, tile_width)
    got_slot = got_slot.reshape(sources * capacity)
    finder = got_slot[None, :] == order[:, None]
    source_row = jnp.sum(jnp.where(finder, every_row[None, :], 0), axis=1)
    residual_tiles = got_res[source_row][:, None]
    new_amplitudes = got_upd[source_row][:, None]
    return (residual_tiles, new_amplitudes)


def solution(mesh):
    return jax.shard_map(
        body,
        mesh=mesh,
        in_specs=(
            P(("groups", "occ"), None, "vir", None),
            P(("groups", "occ"), "vir"),
            P(("groups", "vir"), None, None, None),
            P(("groups", "vir"), None),
            P(("groups", "vir"), None, None),
            P(("groups", "occ"), None, None),
            P(("groups", "occ"), None),
            P(("groups", "vir"), None),
            P(("groups", "occ"), "vir"),
            P(("groups", "occ"), "vir"),
        ),
        out_specs=(
            P(("groups", "occ"), "vir", None, None),
            P(("groups", "occ"), "vir", None, None),
        ),
        check_vma=False,
    )
```

profile of v0, /device:TPU:0, one launch (start us, length us, event | category | flops | bytes accessed | tf_op | source)
XLA Modules:
  0.0 440.1 jit_solution(3546667977272914629)
XLA Ops:
  7.2 0.8 convert_element_type.27
  8.0 0.1 copy.43
  8.1 0.8 convert_element_type.26
  9.0 2.1 copy_multiply_fusion
  11.1 0.1 copy-done.3
  11.2 0.4 broadcast_multiply_fusion
  11.6 1.1 copy-done.2
  12.7 11.1 %convolution_bitcast_fusion = f32[24,1600,128]{2,1,0:T(8,128)} fusion(bf16[1600,6,128,1]{2,0,1,3:T(8,128)(2,1)S(1)} %bitcast.57, bf16[6,128,24,128]{3,2,1,0:T(8,128)(2,1)S(1)} %broadcast_multiply_fusion), kind=kOutput, calls=%fused_computation.5 | convolution fusion | flops 7549747200 | bytes 26836992 | tf_op jit(solution)/shard_map/rkc,kcAa->Ara/dot_general | solution.py:27
  23.9 0.7 copy-done.5
  24.5 0.1 copy.39
  24.9 0.1 copy.38
  25.1 0.2 convert_reduce_fusion
  25.3 0.2 fusion.5
  25.7 0.7 gather_fusion.1
  26.6 0.2 and_reduce_fusion
  26.8 0.7 copy.49
  27.5 6.3 %all-to-all-start.1 = ((s32[4,1,6]{2,1,0:T(1,128)}), s32[4,1,6]{2,1,0:T(1,128)S(1)}, u32[]{:S(2)}, u32[]{:S(2)}) async-start(s32[4,1,6]{2,1,0:T(1,128)} %copy.49), calls=%async_computation.2 | async-start | bytes 4096 | tf_op jit(solution)/shard_map/all_to_all | solution.py:60
  33.8 0.1 copy.41
  34.0 6.3 %fusion.3 = f32[6,4,400,128]{3,2,1,0:T(8,128)} fusion(bf16[4,400,6,128]{3,1,0,2:T(8,128)(2,1)} %copy-done.2, bf16[6,128,128]{2,1,0:T(8,128)(2,1)S(1)} %copy-done.4), kind=kOutput, calls=%fused_computation.15 | convolution fusion | flops 314572800 | bytes 7569408 | tf_op jit(solution)/shard_map/prAc,Aca->Apra/dot_general | solution.py:33
  40.3 131.0 %reduce-scatter.2.cloned.1.call-done = f32[6,1600,128]{2,1,0:T(8,128)} async-done(((f32[24,1600,128]{2,1,0:T(8,128)}), f32[6,1600,128]{2,1,0:T(8,128)}) %reduce-scatter.2.cloned.1.call-update) | async-done | bytes 4915216 | tf_op jit(solution)/shard_map/reduce_scatter | solution.py:26
  171.3 8.8 %bitcast_add_fusion = (f32[6,4,400,128]{3,2,1,0:T(8,128)}, f32[6,4,400,128]{3,2,1,0:T(8,128)}) fusion(bf16[4,400,6,128]{3,1,0,2:T(8,128)(2,1)} %copy-done.2, f32[4,400]{1,0:T(4,128)S(1)} %copy-done.7, f32[6,128]{1,0:T(8,128)S(1)} %copy-done.8, bf16[4,400,400]{2,1,0:T(8,128)(2,1)S(1)} %copy-done, f32[6,4,400,128]{3,2,1,0:T(8,128)} %bitcast.62, ...), kind=kOutput, calls=%fused_computation.6 | convolution fusion | flops 991641600 | bytes 23407968 | tf_op jit(solution)/shard_map/prs,psAa->Apra/dot_general | solution.py:34
  180.1 5.4 %gather_fusion.3 = f32[24,400,128]{2,1,0:T(8,128)} fusion(f32[24,400,128]{2,1,0:T(8,128)} %bitcast.61, s32[1024]{0:T(1024)S(1)} %pad_clamp_fusion.1), kind=kCustom, calls=%fused_computation.3 | custom fusion | bytes 9830496 | tf_op jit(solution)/shard_map/gather | solution.py:55
  185.5 5.5 %gather_fusion = f32[24,400,128]{2,1,0:T(8,128)} fusion(f32[24,400,128]{2,1,0:T(8,128)} %bitcast.60, s32[1024]{0:T(1024)S(1)} %pad_clamp_fusion.1), kind=kCustom, calls=%fused_computation | custom fusion | bytes 9830496 | tf_op jit(solution)/shard_map/gather | solution.py:50
  191.0 8.7 %broadcast_select_fusion = (f32[4,6,400,128]{3,2,1,0:T(8,128)}, f32[4,6,400,128]{3,2,1,0:T(8,128)}) fusion(f32[4,6,400,128]{3,2,1,0:T(8,128)} %bitcast.55, pred[4,6]{1,0:T(4,128)(4,1)S(1)} %copy.41, f32[4,6,400,128]{3,2,1,0:T(8,128)} %bitcast.56), kind=kLoop, calls=%fused_computation.11 | loop fusion | flops 2457600 | bytes 19660824 | tf_op jit(solution)/shard_map/jit(_where)/select_n | solution.py:55
  199.7 114.9 %all_to_all.16 = f32[4,6,400,128]{3,2,1,0:T(8,128)} all-to-all(f32[4,6,400,128]{3,2,1,0:T(8,128)} %get-tuple-element.5), channel_id=1, replica_groups=mesh['groups'=2,'occ'=4,'vir'=4] {'occ'}, dimensions={0} | all-to-all | bytes 9830400 | tf_op jit(solution)/shard_map/all_to_all | solution.py:58
  314.6 5.0 %all-to-all-start.2 = ((f32[4,6,400,128]{3,2,1,0:T(8,128)}), f32[4,6,400,128]{3,2,1,0:T(8,128)}, u32[]{:S(2)}, u32[]{:S(2)}) async-start(f32[4,6,400,128]{3,2,1,0:T(8,128)} %get-tuple-element.4), calls=%async_computation.3 | async-start | bytes 9830400 | tf_op jit(solution)/shard_map/all_to_all | solution.py:59
  319.5 0.5 broadcast.181
  320.1 0.7 reduce.3
  320.8 0.1 select_reduce_fusion
  320.9 5.5 %gather_fusion.2 = f32[24,400,128]{2,1,0:T(8,128)} fusion(f32[24,400,128]{2,1,0:T(8,128)} %bitcast.54, s32[1024]{0:T(1024)S(1)} %pad_clamp_fusion), kind=kCustom, calls=%fused_computation.2 | custom fusion | bytes 9830496 | tf_op jit(solution)/shard_map/gather | solution.py:67
  326.4 101.2 %all-to-all-done.2 = f32[4,6,400,128]{3,2,1,0:T(8,128)} async-done(((f32[4,6,400,128]{3,2,1,0:T(8,128)}), f32[4,6,400,128]{3,2,1,0:T(8,128)}, u32[]{:S(2)}, u32[]{:S(2)}) %all-to-all-start.2) | async-done | bytes 4915232 | tf_op jit(solution)/shard_map/all_to_all | solution.py:59
  427.7 5.6 %gather_fusion.4 = f32[24,400,128]{2,1,0:T(8,128)} fusion(f32[24,400,128]{2,1,0:T(8,128)} %bitcast.25, s32[1024]{0:T(1024)S(1)} %pad_clamp_fusion), kind=kCustom, calls=%fused_computation.4 | custom fusion | bytes 9830496 | tf_op jit(solution)/shard_map/gather | solution.py:68
  (39 shorter events, 1.1 us)
Async XLA Ops:
  7.2 164.1 %copy-start = (bf16[4,400,400]{2,1,0:T(8,128)(2,1)S(1)}, bf16[4,400,400]{2,1,0:T(8,128)(2,1)}, u32[]{:S(2)}) copy-start(bf16[4,400,400]{2,1,0:T(8,128)(2,1)} %param.15) | copy-start | bytes 3840004
  7.2 164.1 %reduce-scatter.2.cloned.1.call-start = ((), (), s32[]{:S(2)}) async-start(), calls=%async_computation.4 | async-start | bytes 24576000 | tf_op jit(solution)/shard_map/reduce_scatter | solution.py:26
  8.1 3.1 copy-start.3
  11.2 1.5 copy-start.2
  23.8 0.7 copy-start.5
  23.8 10.1 %copy-start.6 = (s32[4,6]{1,0:T(4,128)S(1)}, s32[4,6]{1,0:T(4,128)}, u32[]{:S(2)}) copy-start(s32[4,6]{1,0:T(4,128)} %param.18) | copy-start | bytes 292
  23.8 10.2 %copy-start.4 = (bf16[6,128,128]{2,1,0:T(8,128)(2,1)S(1)}, bf16[6,128,128]{2,1,0:T(8,128)(2,1)}, u32[]{:S(2)}) copy-start(bf16[6,128,128]{2,1,0:T(8,128)(2,1)} %param.14) | copy-start | bytes 589828
  24.5 146.8 %copy-start.7 = (f32[4,400]{1,0:T(4,128)S(1)}, f32[4,400]{1,0:T(4,128)}, u32[]{:S(2)}) copy-start(f32[4,400]{1,0:T(4,128)} %param.16) | copy-start | bytes 19204
  24.5 146.8 %copy-start.8 = (f32[6,128]{1,0:T(8,128)S(1)}, f32[6,128]{1,0:T(8,128)}, u32[]{:S(2)}) copy-start(f32[6,128]{1,0:T(8,128)} %param.17) | copy-start | bytes 9220
  27.5 172.2 %all-to-all-start.1 = ((s32[4,1,6]{2,1,0:T(1,128)}), s32[4,1,6]{2,1,0:T(1,128)S(1)}, u32[]{:S(2)}, u32[]{:S(2)}) async-start(s32[4,1,6]{2,1,0:T(1,128)} %copy.49), calls=%async_computation.2 | async-start | bytes 4096 | tf_op jit(solution)/shard_map/all_to_all | solution.py:60
  314.6 113.1 %all-to-all-start.2 = ((f32[4,6,400,128]{3,2,1,0:T(8,128)}), f32[4,6,400,128]{3,2,1,0:T(8,128)}, u32[]{:S(2)}, u32[]{:S(2)}) async-start(f32[4,6,400,128]{3,2,1,0:T(8,128)} %get-tuple-element.4), calls=%async_computation.3 | async-start | bytes 9830400 | tf_op jit(solution)/shard_map/all_to_all | solution.py:59
  427.7 5.6 %copy-start.1 = (bf16[4,400,400]{2,1,0:T(8,128)(2,1)S(1)}, bf16[4,400,400]{2,1,0:T(8,128)(2,1)}, u32[]{:S(2)}) copy-start(bf16[4,400,400]{2,1,0:T(8,128)(2,1)} %param.15) | copy-start | bytes 3840004
Sparse Core Ops, SparseCore 0:
  24.0 147.2 reduce-scatter.1
where the time goes:
time: 441 us; the launch traced here: 440 us
  waiting for transfers between devices  232 us (53%)
  blocking collectives  115 us (26%)
  local copies, waits for them, and re-layouts  27.2 us (6%)
  matrix products  26.2 us (6%)
  other arithmetic  14.2 us (3%)
  between operations  14.1 us (3%)
  starting transfers between devices  11.3 us (3%)
    reduce_scatter x1, waiting for transfers between devices, body(): lax.psum_scatter(jnp.einsum('rkc,kcAa->Ara', flat_amps, masked_ints, pref...  131 us
    all_to_all x1, blocking collectives, body(): lax.all_to_all(send_res, 'occ', split_axis=0, concat_axis=0, tiled=True)  115 us
    all_to_all x1, waiting for transfers between devices, body(): lax.all_to_all(send_upd, 'occ', split_axis=0, concat_axis=0, tiled=True)  101 us
    dot_general x1, matrix products, body(): jnp.einsum('rkc,kcAa->Ara', flat_amps, masked_ints, preferred_element_typ...  11.1 us
  transfers between devices with their start and end apart: 3, of which 2 were waited for; matrix products, arithmetic and copies ran while one was open for 10% of the time, Pallas kernels for 0%

commit v1 on v0

v1 whole, which is shorter than its diff:
```python
import functools

import jax
import jax.numpy as jnp
from jax import lax
from jax.experimental import pallas as pl
from jax.experimental.pallas import tpu as pltpu
from jax.sharding import PartitionSpec as P

CODE_ROWS = 16
LEVELS = 32700.0
VMEM_BYTES = 48 * 1024 * 1024
ANY = pl.BlockSpec(memory_space=pl.ANY)


def params():
    return pltpu.CompilerParams(vmem_limit_bytes=VMEM_BYTES)


def held(array):
    rank = len(array.shape)
    return pl.BlockSpec(array.shape, lambda i, table: (0,) * rank, pipeline_mode=pl.Buffered(1))


def scale_block(rows):
    return 80 if rows % 80 == 0 else rows


def encode(values, out_ref):
    rows, width = values.shape
    block = scale_block(rows)
    cut = values.reshape(rows // block, block, width)
    top = jnp.max(jnp.abs(cut), axis=1, keepdims=True)
    step = jnp.clip(jnp.ceil(8.0 * jnp.log2(jnp.maximum(top, 1e-30))), -800.0, 800.0)
    whole = jnp.round(cut * (LEVELS * jnp.exp2(step * -0.125))).reshape(rows, width)
    out_ref[0, :rows, :] = whole.astype(jnp.int32).astype(jnp.int16)
    steps = step.reshape(rows // block, width)
    steps = jnp.concatenate([steps, jnp.zeros((CODE_ROWS - rows // block, width), jnp.float32)], axis=0)
    out_ref[0, rows:, :] = steps.astype(jnp.int32).astype(jnp.int16)


def decode(coded):
    rows, width = coded.shape[0] - CODE_ROWS, coded.shape[1]
    block = scale_block(rows)
    steps = coded[rows:, :].astype(jnp.int32).astype(jnp.float32)[: rows // block]
    scale = jnp.exp2(steps * 0.125) * (1.0 / LEVELS)
    whole = coded[:rows, :].astype(jnp.int32).astype(jnp.float32)
    return (whole.reshape(rows // block, block, width) * scale.reshape(rows // block, 1, width)).reshape(rows, width)


def add_ladder(total, table, base, tile, blocks, runs, run, amps_own, amps_other, ints_own, ints_other):
    pair, column = tile // blocks, tile % blocks
    tiles = amps_own.shape[0]
    ints_len = blocks * runs * blocks
    for part, (amps, ints) in enumerate(((amps_own, ints_own), (amps_other, ints_other))):
        amp_base = base + part * tiles
        int_base = base + 2 * tiles + part * ints_len

        def step(block, carry):
            source = pair * blocks + block
            kept = table[amp_base + source] * table[int_base + (block * runs + run) * blocks + column]

            @pl.when(kept != 0)
            def _():
                total[...] += jnp.dot(amps[source], ints[run, column, block], preferred_element_type=jnp.float32)

            return carry

        lax.fori_loop(0, blocks, step, 0)


def sums_kernel(blocks, runs, per_chunk, chunks, table, amps_own, amps_other, ints_own, ints_other, *refs):
    outs, total = refs[:chunks], refs[chunks]
    entries = per_chunk * chunks
    i = pl.program_id(0)
    tile = table[i]

    @pl.when(tile >= 0)
    def _():
        total[...] = jnp.zeros_like(total)
        run = table[entries]
        add_ladder(total, table, entries + 1, tile, blocks, runs, run, amps_own, amps_other, ints_own, ints_other)
        for chunk in range(chunks):

            @pl.when(i // per_chunk == chunk)
            def _():
                encode(total[...], outs[chunk])


def own_kernel(
    blocks, runs, entries, table, amps_own, amps_other, ints_own, ints_other, fock_vir, fock_occ, out, total
):
    tile = table[pl.program_id(0)]

    @pl.when(tile >= 0)
    def _():
        total[...] = jnp.zeros_like(total)
        run = table[entries]
        add_ladder(total, table, entries + 1, tile, blocks, runs, run, amps_own, amps_other, ints_own, ints_other)

        @pl.when(table[entries + 1 + tile] != 0)
        def _():
            amps = amps_own[tile]
            total[...] += jnp.dot(amps, fock_vir[tile % blocks], preferred_element_type=jnp.float32)
            total[...] -= jnp.dot(fock_occ[tile // blocks], amps, preferred_element_type=jnp.float32)

        out[0] = total[...]


def join_kernel(others, per_dest, dests, first, table, own, *refs):
    came, outs = refs[:others], refs[others:]
    i = pl.program_id(0)

    @pl.when(table[first + i] >= 0)
    def _():
        total = own[0]
        for ref in came:
            total = total + decode(ref[0])
        for dest in range(dests):

            @pl.when(i // per_dest == dest)
            def _():
                encode(total, outs[dest])


def pack_kernel(dests, slots, table, amps, *refs):
    outs, sem = refs[:dests], refs[dests]
    copies = [
        pltpu.make_async_copy(amps.at[table[dest * slots + slot]], outs[dest].at[slot], sem.at[dest * slots + slot])
        for dest in range(dests)
        for slot in range(slots)
    ]
    for copy in copies:
        copy.start()
    for copy in copies:
        copy.wait()


def final_kernel(chunks, dests, per_dest, table, occ_cols, vir_energy, *refs):
    codes = refs[: chunks * dests]
    amps = refs[chunks * dests : chunks * dests + dests]
    out_res, out_upd, held_codes, held_amps, sem = refs[chunks * dests + dests :]
    slot = pl.program_id(0)
    slots_all = pl.num_programs(0)

    @pl.when(slot == 0)
    def _():
        copies = []
        for n, ref in enumerate(codes):
            copies.append(
                pltpu.make_async_copy(ref, held_codes.at[pl.ds(n * per_dest, per_dest)], sem.at[n])
            )
        many = chunks * per_dest
        for n, ref in enumerate(amps):
            copies.append(
                pltpu.make_async_copy(ref, held_amps.at[pl.ds(n * many, many)], sem.at[len(codes) + n])
            )
        for copy in copies:
            copy.start()
        for copy in copies:
            copy.wait()

    def entry(row):
        return table[row * slots_all + slot]

    rows, width = out_res.shape[2], out_res.shape[3]
    res_kept, amp_kept = entry(4) != 0, entry(5) != 0
    resid = jnp.where(res_kept, decode(held_codes[entry(0)]), 0.0)
    kept = jnp.where(amp_kept, held_amps[entry(1)].astype(jnp.float32), 0.0)
    lane = lax.broadcasted_iota(jnp.int32, (rows, width), 1)
    occ = jnp.sum(jnp.where(lane == entry(2), occ_cols[...], 0.0), axis=1, keepdims=True)
    vir = vir_energy[pl.ds(entry(3), 1), :]
    out_res[0, 0] = resid
    out_upd[0, 0] = kept + resid / (vir - occ)


def body(
    amplitudes,
    amp_keep,
    integrals,
    int_keep,
    fock_vir,
    fock_occ,
    occ_energy,
    vir_energy,
    res_keep,
    res_place,
):
    pairs, rows, blocks, width = amplitudes.shape
    dests, virs = lax.axis_size("occ"), lax.axis_size("vir")
    runs = virs // 2
    me_occ, me_vir = lax.axis_index("occ"), lax.axis_index("vir")
    core, chip = me_vir % 2, me_vir // 2
    tiles = pairs * blocks
    slots = max(2, (tiles + dests - 1) // dests)
    chunks = 3 if slots % 3 == 0 else slots
    per_dest = slots // chunks
    per_chunk = per_dest * dests
    entries = chunks * per_chunk
    coded_rows = rows + CODE_ROWS

    def swap(array, axis, bit):
        size = lax.axis_size(axis)
        return lax.ppermute(array, axis, [(i, i ^ bit) for i in range(size)])

    places = res_place.reshape(tiles)
    res_kept = res_keep.reshape(tiles)
    amp_kept = amp_keep.reshape(tiles)
    toward = (places // tiles) ^ me_occ
    order = jnp.arange(tiles, dtype=jnp.int32)
    key = order + jnp.where(res_kept != 0, 0, tiles)
    earlier = (toward[None, :] == toward[:, None]) & (key[None, :] < key[:, None])
    rank = jnp.sum(earlier.astype(jnp.int32), axis=1)
    match = (toward[None, None, :] == jnp.arange(dests, dtype=jnp.int32)[:, None, None]) & (
        rank[None, None, :] == jnp.arange(slots, dtype=jnp.int32)[None, :, None]
    )
    fields = jnp.stack([places % tiles + 1, order, res_kept, amp_kept])
    meta = jnp.sum(jnp.where(match[None], fields[:, None, None, :], 0), axis=3)
    slot_tile = meta[1]
    todo = jnp.where((meta[0] > 0) & (meta[2] != 0), slot_tile, -1)
    todo = jnp.transpose(todo.reshape(dests, chunks, per_dest), (1, 0, 2)).reshape(entries)
    todo_other = [swap(todo, "vir", 2 * k) for k in range(1, runs)]

    amps = jnp.transpose(amplitudes, (0, 2, 1, 3)).reshape(tiles, rows, width)

    packed = pl.pallas_call(
        functools.partial(pack_kernel, dests, slots),
        out_shape=[jax.ShapeDtypeStruct((slots, rows, width), amps.dtype)] * dests,
        grid_spec=pltpu.PrefetchScalarGridSpec(
            num_scalar_prefetch=1,
            grid=(1,),
            in_specs=[ANY],
            out_specs=[ANY] * dests,
            scratch_shapes=[pltpu.SemaphoreType.DMA((dests * slots,))],
        ),
        compiler_params=params(),
        cost_estimate=pl.CostEstimate(flops=0, bytes_accessed=4 * amps.size, transcendentals=0),
        name="pack_amps",
    )(slot_tile.reshape(dests * slots), amps)
    amps_came = [packed[0]] + [swap(packed[s], "occ", s) for s in range(1, dests)]

    by_core = jnp.transpose(integrals.reshape(blocks, width, runs, 2, blocks, width), (3, 2, 4, 0, 1, 5))
    ints_own = lax.dynamic_index_in_dim(by_core, core, 0, keepdims=False)
    ints_other = swap(lax.dynamic_index_in_dim(by_core, 1 - core, 0, keepdims=False), "vir", 1)
    amps_other = swap(amps, "vir", 1)
    keep_by_core = jnp.transpose(int_keep.reshape(blocks, runs, 2, blocks), (2, 0, 1, 3)).reshape(2, -1)
    keep_own = lax.dynamic_index_in_dim(keep_by_core, core, 0, keepdims=False)
    keep_send = lax.dynamic_index_in_dim(keep_by_core, 1 - core, 0, keepdims=False)
    keep_came = swap(jnp.concatenate([amp_kept, keep_send]), "vir", 1)
    keeps = jnp.concatenate([amp_kept, keep_came[:tiles], keep_own, keep_came[tiles:]])

    shared = (amps, amps_other, ints_own, ints_other)
    share_specs = [held(a) for a in shared]
    flops = 2 * tiles * rows * width * width
    tile_bytes = rows * width

    def clamped(first, count):
        return lambda i, table: (jnp.clip(i - first, 0, count - 1), 0, 0)

    sums_came = []
    for k in range(1, runs):
        sums = pl.pallas_call(
            functools.partial(sums_kernel, blocks, runs, per_chunk, chunks),
            out_shape=[jax.ShapeDtypeStruct((per_chunk, coded_rows, width), jnp.int16)] * chunks,
            grid_spec=pltpu.PrefetchScalarGridSpec(
                num_scalar_prefetch=1,
                grid=(entries,),
                in_specs=share_specs,
                out_specs=[
                    pl.BlockSpec((1, coded_rows, width), clamped(c * per_chunk, per_chunk)) for c in range(chunks)
                ],
                scratch_shapes=[pltpu.VMEM((rows, width), jnp.float32)],
            ),
            compiler_params=params(),
            cost_estimate=pl.CostEstimate(flops=4 * flops, bytes_accessed=8 * tiles * tile_bytes, transcendentals=0),
            name="ladder_sums",
        )(jnp.concatenate([todo_other[k - 1], (chip ^ k)[None], keeps]), *shared)
        sums_came.append([swap(sums[c], "vir", 2 * k) for c in range(chunks)])

    own = pl.pallas_call(
        functools.partial(own_kernel, blocks, runs, entries),
        out_shape=jax.ShapeDtypeStruct((entries, rows, width), jnp.float32),
        grid_spec=pltpu.PrefetchScalarGridSpec(
            num_scalar_prefetch=1,
            grid=(entries,),
            in_specs=share_specs + [held(fock_vir), held(fock_occ)],
            out_specs=pl.BlockSpec((1, rows, width), lambda i, table: (i, 0, 0)),
            scratch_shapes=[pltpu.VMEM((rows, width), jnp.float32)],
        ),
        compiler_params=params(),
        cost_estimate=pl.CostEstimate(flops=4 * flops, bytes_accessed=10 * tiles * tile_bytes, transcendentals=0),
        name="own_part",
    )(jnp.concatenate([todo, chip[None], keeps]), *shared, fock_vir, fock_occ)

    codes = []
    for c in range(chunks):
        first = c * per_chunk
        joined = pl.pallas_call(
            functools.partial(join_kernel, runs - 1, per_dest, dests, first),
            out_shape=[jax.ShapeDtypeStruct((per_dest, coded_rows, width), jnp.int16)] * dests,
            grid_spec=pltpu.PrefetchScalarGridSpec(
                num_scalar_prefetch=1,
                grid=(per_chunk,),
                in_specs=[pl.BlockSpec((1, rows, width), lambda i, table, first=first: (first + i, 0, 0))]
                + [pl.BlockSpec((1, coded_rows, width), lambda i, table: (i, 0, 0))] * (runs - 1),
                out_specs=[pl.BlockSpec((1, coded_rows, width), clamped(s * per_dest, per_dest)) for s in range(dests)],
            ),
            compiler_params=params(),
            cost_estimate=pl.CostEstimate(
                flops=10 * per_chunk * tile_bytes, bytes_accessed=8 * per_chunk * tile_bytes, transcendentals=0
            ),
            name="join_parts",
        )(todo, own, *[came[c] for came in sums_came])
        codes += [joined[0]] + [swap(joined[s], "occ", s) for s in range(1, dests)]

    notes = [jnp.concatenate([occ_energy.reshape(-1), meta[:, s].reshape(-1).astype(jnp.float32)]) for s in range(dests)]
    notes = jnp.stack([notes[0]] + [swap(notes[s], "occ", s) for s in range(1, dests)])
    occ_all = notes[:, : pairs * rows].reshape(dests * pairs, rows)
    occ_cols = jnp.transpose(jnp.pad(occ_all, ((0, width - dests * pairs), (0, 0))))
    info = notes[:, pairs * rows :].astype(jnp.int32).reshape(dests, 4, slots)
    source = jnp.arange(dests, dtype=jnp.int32)[:, None]
    place = jnp.arange(slots, dtype=jnp.int32)[None, :]
    code_at = (place // per_dest) * per_chunk + source * per_dest + place % per_dest
    amps_at = source * slots + place
    columns = jnp.stack([code_at, amps_at, source * pairs + info[:, 1] // blocks, info[:, 1] % blocks, info[:, 2], info[:, 3]])
    here = info[:, 0][None] == jnp.arange(1, tiles + 1, dtype=jnp.int32)[:, None, None]
    table = jnp.sum(jnp.where(here[None], columns[:, None], 0), axis=(2, 3)).reshape(-1)

    return pl.pallas_call(
        functools.partial(final_kernel, chunks, dests, per_dest),
        out_shape=[jax.ShapeDtypeStruct((tiles, 1, rows, width), jnp.float32)] * 2,
        grid_spec=pltpu.PrefetchScalarGridSpec(
            num_scalar_prefetch=1,
            grid=(tiles,),
            in_specs=[held(occ_cols), held(vir_energy)] + [ANY] * (chunks * dests + dests),
            out_specs=[pl.BlockSpec((1, 1, rows, width), lambda i, table: (i, 0, 0, 0))] * 2,
            scratch_shapes=[
                pltpu.VMEM((entries, coded_rows, width), jnp.int16),
                pltpu.VMEM((entries, rows, width), jnp.bfloat16),
                pltpu.SemaphoreType.DMA((chunks * dests + dests,)),
            ],
        ),
        compiler_params=params(),
        cost_estimate=pl.CostEstimate(
            flops=10 * tiles * tile_bytes, bytes_accessed=12 * tiles * tile_bytes, transcendentals=0
        ),
        name="update_tiles",
    )(table, occ_cols, vir_energy, *codes, *amps_came)


def solution(mesh):
    return jax.shard_map(
        body,
        mesh=mesh,
        in_specs=(
            P(("groups", "occ"), None, "vir", None),
            P(("groups", "occ"), "vir"),
            P(("groups", "vir"), None, None, None),
            P(("groups", "vir"), None),
            P(("groups", "vir"), None, None),
            P(("groups", "occ"), None, None),
            P(("groups", "occ"), None),
            P(("groups", "vir"), None),
            P(("groups", "occ"), "vir"),
            P(("groups", "occ"), "vir"),
        ),
        out_specs=(
            P(("groups", "occ"), "vir", None, None),
            P(("groups", "occ"), "vir", None, None),
        ),
        check_vma=False,
    )
```

time: 441 us -> 185 us (0.42)
  waiting for transfers between devices: 232 us -> 51.5 us
  blocking collectives: 115 us -> 0 us
  Pallas kernels: 0 us -> 73.4 us
  matrix products: 26.2 us -> 0 us
  starting transfers between devices: 11.3 us -> 29.6 us
  between operations: 14.1 us -> 0.93 us
  other arithmetic: 14.2 us -> 1.5 us
    reduce_scatter x1 -> x0, waiting for transfers between devices: 131 us -> none  [body(): lax.psum_scatter(jnp.einsum('rkc,kcAa->Ara', flat_amps, masked_ints, pref...]
    all_to_all x1 -> x0, blocking collectives: 115 us -> none  [body(): lax.all_to_all(send_res, 'occ', split_axis=0, concat_axis=0, tiled=True)]
    all_to_all x2 -> x0, waiting for transfers between devices: 101 us -> none  [the longest x1 101 us: body(): lax.all_to_all(send_upd, 'occ', split_axis=0, concat_axis=0, tiled=True)]
    pallas_call x0 -> x7, Pallas kernels: none -> 73.4 us  [the longest x1 18.1 us: body(): pl.pallas_call(functools.partial(sums_kernel, blocks, runs, per_chunk, ch...]
    ppermute x0 -> x22, waiting for transfers between devices: none -> 51.5 us  [swap(): return lax.ppermute(array, axis, [(i, i ^ bit) for i in range(size)])]
    ppermute x0 -> x22, starting transfers between devices: none -> 29.6 us  [swap(): return lax.ppermute(array, axis, [(i, i ^ bit) for i in range(size)])]
    dot_general x3 -> x0, matrix products: 26.2 us -> none  [the longest x1 11.1 us: body(): jnp.einsum('rkc,kcAa->Ara', flat_amps, masked_ints, preferred_element_typ...]
    gather x7 -> x0, local copies, waits for them, and re-layouts: 23 us -> none  [the longest x1 5.63 us: body(): new_amplitudes = got_upd[source_row][:, None]]
  transfers between devices with their start and end apart: 3 -> 22, of which waited for: 2 -> 5; matrix products, arithmetic and copies ran while one was open for 10% -> 5% of each run, Pallas kernels for 0% -> 31%
where the time goes in v1:
time: 185 us; the launch traced here: 182 us
  Pallas kernels  73.4 us (40%)
  waiting for transfers between devices  51.5 us (28%)
  starting transfers between devices  29.6 us (16%)
  local copies, waits for them, and re-layouts  25.3 us (14%)
    ppermute x22, waiting for transfers between devices, swap(): return lax.ppermute(array, axis, [(i, i ^ bit) for i in range(size)])  51.5 us
    ppermute x22, starting transfers between devices, swap(): return lax.ppermute(array, axis, [(i, i ^ bit) for i in range(size)])  29.6 us
    pallas_call x1, Pallas kernels, body(): pl.pallas_call(functools.partial(sums_kernel, blocks, runs, per_chunk, ch...  18.1 us
    pallas_call x1, Pallas kernels, body(): pl.pallas_call(functools.partial(own_kernel, blocks, runs, entries), out_...  17.7 us
    pallas_call x3, Pallas kernels, body(): pl.pallas_call(functools.partial(join_kernel, runs - 1, per_dest, dests,...  17.2 us
    pallas_call x1, Pallas kernels, body(): pl.pallas_call(functools.partial(final_kernel, chunks, dests, per_dest),...  16.1 us
    unnamed x36, local copies, waits for them, and re-layouts  15.8 us
    another operation x1, local copies, waits for them, and re-layouts  5.15 us
  transfers between devices with their start and end apart: 22, of which 5 were waited for; matrix products, arithmetic and copies ran while one was open for 5% of the time, Pallas kernels for 31%

profile of v1, /device:TPU:0, one launch (start us, length us, event | category | flops | bytes accessed | tf_op | source)
XLA Modules:
  0.0 182.3 jit_solution(15716939168909273872)
XLA Ops:
  0.6 5.8 %copy.52 = bf16[6,128,24,128]{3,1,2,0:T(8,128)(2,1)} copy(bf16[6,128,24,128]{3,2,1,0:T(8,128)(2,1)} %param.12) | data formatting | bytes 9437184 | tf_op args[2]
  6.4 5.2 %constant_dynamic-slice_fusion = (bf16[6,128,2,1,6,128]{5,1,4,3,2,0:T(8,128)(2,1)S(1)}, bf16[6,128,2,1,6,128]{5,1,4,3,2,0:T(8,128)(2,1)}) fusion(bf16[6,128,2,2,6,128]{5,1,4,3,2,0:T(8,128)(2,1)} %bitcast.42, s32[]{:T(128)S(6)} %select_n.142, s32[]{:T(128)S(6)} %select_n.143), kind=kLoop, calls=%fused_computation.54 | loop fusion | bytes 9437192 | tf_op jit(solution)/shard_map/dynamic-slice.1
  11.6 1.6 copy.61
  16.2 2.6 %collective-permute-start.6 = (s32[24]{0:T(128)S(1)}, s32[24]{0:T(128)S(1)}, u32[]{:S(2)}, u32[]{:S(2)}) collective-permute-start(s32[24]{0:T(128)S(1)} %reshape.489.table), channel_id=1, source_target_pairs={{0,2},{1,3},{2,0},{3,1},{4,6},{5,7},{6,4},{7,5},{8,10},{9,11},{10,... | collective-permute-start | bytes 296 | tf_op jit(solution)/shard_map/ppermute | solution.py:204
  19.4 1.6 collective-permute-start
  21.1 2.7 %collective-permute-start.1 = (f32[1624]{0:T(1024)S(1)}, f32[1624]{0:T(1024)S(1)}, u32[]{:S(2)}, u32[]{:S(2)}) collective-permute-start(f32[1624]{0:T(1024)S(1)} %get-tuple-element.55), channel_id=1, source_target_pairs={{0,8},{4,12},{8,0},{12,4},{1,9},{5,13},{9,1},{13,5},{2,10},{6,14},... | collective-permute-start | bytes 19496 | tf_op jit(solution)/shard_map/ppermute | solution.py:204
  23.8 1.0 collective-permute-start.2
  24.8 3.4 %copy.62 = bf16[6,128,2,1,6,128]{5,1,0,4,2,3:T(8,128)(2,1)} copy(bf16[6,128,2,1,6,128]{5,1,4,3,2,0:T(8,128)(2,1)} %get-tuple-element.45) | data formatting | bytes 4718592
  28.3 4.3 %pack_amps.1 = (bf16[6,400,128]{2,1,0:T(8,128)(2,1)S(1)}, bf16[6,400,128]{2,1,0:T(8,128)(2,1)S(1)}, bf16[6,400,128]{2,1,0:T(8,128)(2,1)S(1)}, bf16[6,400,128]{2,1,0:T(8,128)(2,1)S(1)}) custom-call(s32[24]{0:T(128)S(1)} %reshape_squeeze.2.table, bf16[24,400,128]{2,1,0:T(8,128)(2,1)S(1)} %bitcast.39), custom_call_target="tpu_custom_call" | custom-call | bytes 4915200 | tf_op jit(solution)/shard_map/pack_amps/pallas_call | solution.py:226
  32.6 0.9 copy-done.4
  35.0 3.2 %collective-permute-start.20 = (bf16[6,400,128]{2,1,0:T(8,128)(2,1)}, bf16[6,400,128]{2,1,0:T(8,128)(2,1)}, u32[]{:S(2)}, u32[]{:S(2)}) collective-permute-start(bf16[6,400,128]{2,1,0:T(8,128)(2,1)} %copy-done.9), channel_id=1, source_target_pairs={{0,8},{4,12},{8,0},{12,4},{1,9},{5,13},{9,1},{13,5},{2,10},{6,14},... | collective-permute-start | bytes 1843208 | tf_op jit(solution)/shard_map/ppermute | solution.py:204
  38.5 1.7 copy-done.1
  40.2 18.1 %ladder_sums.1 = (s16[8,416,128]{2,1,0:T(8,128)(2,1)}, s16[8,416,128]{2,1,0:T(8,128)(2,1)}, s16[8,416,128]{2,1,0:T(8,128)(2,1)}) custom-call(s32[217]{0:T(256)S(1)} %concatenate.30.table, bf16[24,400,128]{2,1,0:T(8,128)(2,1)} %bitcast.36, bf16[24,400,128]{2,1,0:T(8,128)(2,1)} %collective-permute-done.4.amps_other, bf16[2,6,6,128,128]{4,3,2,1,0:T(8,128)(2,1)S(1)} %bitcast.40, ...), custom_call_target="tpu_custom_call" | custom-call | flops 1258291200 | bytes 9830400 | tf_op jit(solution)/shard_map/ladder_sums/pallas_call | solution.py:262
  58.3 2.1 %collective-permute-start.11 = (s16[8,416,128]{2,1,0:T(8,128)(2,1)}, s16[8,416,128]{2,1,0:T(8,128)(2,1)}, u32[]{:S(2)}, u32[]{:S(2)}) collective-permute-start(s16[8,416,128]{2,1,0:T(8,128)(2,1)} %get-tuple-element.26), channel_id=1, source_target_pairs={{0,2},{1,3},{2,0},{3,1},{4,6},{5,7},{6,4},{7,5},{8,10},{9,11},{10,... | collective-permute-start | bytes 2555912 | tf_op jit(solution)/shard_map/ppermute | solution.py:204
  60.8 19.6 %collective-permute-done.15.refs_0_ = s16[8,416,128]{2,1,0:T(8,128)(2,1)} collective-permute-done((s16[8,416,128]{2,1,0:T(8,128)(2,1)}, s16[8,416,128]{2,1,0:T(8,128)(2,1)}, u32[]{:S(2)}, u32[]{:S(2)}) %collective-permute-start.15) | collective-permute-done | bytes 852000 | tf_op jit(solution)/shard_map/ppermute | solution.py:204
  80.6 0.8 copy.49
  81.7 1.4 copy-done.3
  83.1 17.7 %own_part.1.own = f32[24,400,128]{2,1,0:T(8,128)} custom-call(s32[217]{0:T(256)S(1)} %concatenate.29.table, bf16[24,400,128]{2,1,0:T(8,128)(2,1)} %bitcast.37, bf16[24,400,128]{2,1,0:T(8,128)(2,1)} %collective-permute-done.4.amps_other, bf16[2,6,6,128,128]{4,3,2,1,0:T(8,128)(2,1)S(1)} %bitcast.41, ...), custom_call_target="tpu_custom_call" | custom-call | flops 1258291200 | bytes 12288000 | tf_op jit(solution)/shard_map/own_part/pallas_call | solution.py:280
  100.8 4.8 %join_parts.5 = (s16[2,416,128]{2,1,0:T(8,128)(2,1)S(1)}, s16[2,416,128]{2,1,0:T(8,128)(2,1)S(1)}, s16[2,416,128]{2,1,0:T(8,128)(2,1)S(1)}, s16[2,416,128]{2,1,0:T(8,128)(2,1)S(1)}) custom-call(s32[24]{0:T(128)S(1)} %reshape.489.table, f32[24,400,128]{2,1,0:T(8,128)} %own_part.1.own, s16[8,416,128]{2,1,0:T(8,128)(2,1)} %collective-permute-done.15.refs_0_), custom_call_target="tpu_custom_call" | custom-call | flops 4096000 | bytes 3276800 | tf_op jit(solution)/shard_map/join_parts/pallas_call | solution.py:298
  105.6 6.2 %join_parts.4 = (s16[2,416,128]{2,1,0:T(8,128)(2,1)S(1)}, s16[2,416,128]{2,1,0:T(8,128)(2,1)S(1)}, s16[2,416,128]{2,1,0:T(8,128)(2,1)}, s16[2,416,128]{2,1,0:T(8,128)(2,1)}) custom-call(s32[24]{0:T(128)S(1)} %reshape.489.table, f32[24,400,128]{2,1,0:T(8,128)} %own_part.1.own, s16[8,416,128]{2,1,0:T(8,128)(2,1)} %collective-permute-done.11.refs_0_), custom_call_target="tpu_custom_call" | custom-call | flops 4096000 | bytes 3276800 | tf_op jit(solution)/shard_map/join_parts/pallas_call | solution.py:298
  111.8 3.9 %collective-permute-start.17 = (s16[2,416,128]{2,1,0:T(8,128)(2,1)S(1)}, s16[2,416,128]{2,1,0:T(8,128)(2,1)S(1)}, u32[]{:S(2)}, u32[]{:S(2)}) collective-permute-start(s16[2,416,128]{2,1,0:T(8,128)(2,1)S(1)} %get-tuple-element.34), channel_id=1, source_target_pairs={{0,8},{4,12},{8,0},{12,4},{1,9},{5,13},{9,1},{13,5},{2,10},{6,14},... | collective-permute-start | bytes 638984 | tf_op jit(solution)/shard_map/ppermute | solution.py:204
  116.5 6.2 %join_parts.3 = (s16[2,416,128]{2,1,0:T(8,128)(2,1)S(1)}, s16[2,416,128]{2,1,0:T(8,128)(2,1)}, s16[2,416,128]{2,1,0:T(8,128)(2,1)}, s16[2,416,128]{2,1,0:T(8,128)(2,1)}) custom-call(s32[24]{0:T(128)S(1)} %reshape.489.table, f32[24,400,128]{2,1,0:T(8,128)} %own_part.1.own, s16[8,416,128]{2,1,0:T(8,128)(2,1)S(1)} %collective-permute-done.7.refs_0_), custom_call_target="tpu_custom_call" | custom-call | flops 4096000 | bytes 3276800 | tf_op jit(solution)/shard_map/join_parts/pallas_call | solution.py:298
  122.8 3.6 %collective-permute-start.13 = (s16[2,416,128]{2,1,0:T(8,128)(2,1)}, s16[2,416,128]{2,1,0:T(8,128)(2,1)S(1)}, u32[]{:S(2)}, u32[]{:S(2)}) collective-permute-start(s16[2,416,128]{2,1,0:T(8,128)(2,1)} %get-tuple-element.29), channel_id=1, source_target_pairs={{0,8},{4,12},{8,0},{12,4},{1,9},{5,13},{9,1},{13,5},{2,10},{6,14},... | collective-permute-start | bytes 638984 | tf_op jit(solution)/shard_map/ppermute | solution.py:204
  126.4 0.8 collective-permute-start.14
  127.2 11.1 %collective-permute-done.17.refs_10_ = s16[2,416,128]{2,1,0:T(8,128)(2,1)S(1)} collective-permute-done((s16[2,416,128]{2,1,0:T(8,128)(2,1)S(1)}, s16[2,416,128]{2,1,0:T(8,128)(2,1)S(1)}, u32[]{:S(2)}, u32[]{:S(2)}) %collective-permute-start.17) | collective-permute-done | bytes 213024 | tf_op jit(solution)/shard_map/ppermute | solution.py:204
  138.2 2.4 %collective-permute-start.10 = (s16[2,416,128]{2,1,0:T(8,128)(2,1)}, s16[2,416,128]{2,1,0:T(8,128)(2,1)S(1)}, u32[]{:S(2)}, u32[]{:S(2)}) collective-permute-start(s16[2,416,128]{2,1,0:T(8,128)(2,1)} %get-tuple-element.25), channel_id=1, source_target_pairs={{0,12},{4,8},{8,4},{12,0},{1,13},{5,9},{9,5},{13,1},{2,14},{6,10},... | collective-permute-start | bytes 638984 | tf_op jit(solution)/shard_map/ppermute | solution.py:204
  140.6 2.7 %collective-permute-start.8 = (s16[2,416,128]{2,1,0:T(8,128)(2,1)}, s16[2,416,128]{2,1,0:T(8,128)(2,1)S(1)}, u32[]{:S(2)}, u32[]{:S(2)}) collective-permute-start(s16[2,416,128]{2,1,0:T(8,128)(2,1)} %get-tuple-element.23), channel_id=1, source_target_pairs={{0,4},{4,0},{8,12},{12,8},{1,5},{5,1},{9,13},{13,9},{2,6},{6,2},{1... | collective-permute-start | bytes 638984 | tf_op jit(solution)/shard_map/ppermute | solution.py:204
  143.4 0.9 collective-permute-start.9
  144.5 0.9 pad_bitcast_fusion.occ_cols
  145.5 5.9 %collective-permute-done.13.refs_6_ = s16[2,416,128]{2,1,0:T(8,128)(2,1)S(1)} collective-permute-done((s16[2,416,128]{2,1,0:T(8,128)(2,1)}, s16[2,416,128]{2,1,0:T(8,128)(2,1)S(1)}, u32[]{:S(2)}, u32[]{:S(2)}) %collective-permute-start.13) | collective-permute-done | bytes 213024 | tf_op jit(solution)/shard_map/ppermute | solution.py:204
  151.6 14.6 %collective-permute-done.9.refs_2_ = s16[2,416,128]{2,1,0:T(8,128)(2,1)S(1)} collective-permute-done((s16[2,416,128]{2,1,0:T(8,128)(2,1)}, s16[2,416,128]{2,1,0:T(8,128)(2,1)S(1)}, u32[]{:S(2)}, u32[]{:S(2)}) %collective-permute-start.9) | collective-permute-done | bytes 213024 | tf_op jit(solution)/shard_map/ppermute | solution.py:204
  166.2 16.1 %update_tiles.1 = (f32[24,1,400,128]{3,2,1,0:T(8,128)}, f32[24,1,400,128]{3,2,1,0:T(8,128)}) custom-call(s32[144]{0:T(256)S(1)} %reshape.487.table, f32[400,128]{1,0:T(8,128)S(1)} %pad_bitcast_fusion.occ_cols, f32[6,128]{1,0:T(8,128)S(1)} %copy-done.7, s16[2,416,128]{2,1,0:T(8,128)(2,1)S(1)} %get-tuple-element.22.refs_0_, ...), custom_call_target="tpu_custom_call" | custom-call | flops 12288000 | bytes 14745600 | tf_op jit(solution)/shard_map/update_tiles/pallas_call | solution.py:329
  (127 shorter events, 7.5 us)
Async XLA Ops:
  11.6 2.3 %copy-start.12 = (s32[4,6]{1,0:T(4,128)S(1)}, s32[4,6]{1,0:T(4,128)}, u32[]{:S(2)}) copy-start(s32[4,6]{1,0:T(4,128)} %param.11) | copy-start | bytes 292
  11.6 2.6 %copy-start = (bf16[4,400,6,128]{3,1,2,0:T(8,128)(2,1)S(1)}, bf16[4,400,6,128]{3,1,2,0:T(8,128)(2,1)}, u32[]{:S(2)}) copy-start(bf16[4,400,6,128]{3,1,2,0:T(8,128)(2,1)} %param.10) | copy-start | bytes 7372804
  11.6 3.0 %copy-start.11 = (s32[4,6]{1,0:T(4,128)S(1)}, s32[4,6]{1,0:T(4,128)}, u32[]{:S(2)}) copy-start(s32[4,6]{1,0:T(4,128)} %param.19) | copy-start | bytes 292
  11.6 3.0 %copy-start.13 = (s32[4,6]{1,0:T(4,128)S(1)}, s32[4,6]{1,0:T(4,128)}, u32[]{:S(2)}) copy-start(s32[4,6]{1,0:T(4,128)} %param.18) | copy-start | bytes 292
  11.6 7.6 %copy-start.14 = (f32[4,400]{1,0:T(4,128)S(1)}, f32[4,400]{1,0:T(4,128)}, u32[]{:S(2)}) copy-start(f32[4,400]{1,0:T(4,128)} %param.16) | copy-start | bytes 19204
  13.2 25.2 %collective-permute-start.5 = (bf16[2,6,6,128,128]{4,3,2,1,0:T(8,128)(2,1)}, bf16[2,6,6,128,128]{4,3,2,1,0:T(8,128)(2,1)}, u32[]{:S(2)}, u32[]{:S(2)}) collective-permute-start(bf16[2,6,6,128,128]{4,3,2,1,0:T(8,128)(2,1)} %bitcast.33), channel_id=1, source_target_pairs={{0,1},{1,0},{2,3},{3,2},{4,5},{5,4},{6,7},{7,6},{8,9},{9,8},{10,11... | collective-permute-start | bytes 7077896 | tf_op jit(solution)/shard_map/ppermute | solution.py:204
  14.1 9.7 %collective-permute-start.3 = (s32[96]{0:T(128)S(1)}, s32[96]{0:T(128)S(1)}, u32[]{:S(2)}, u32[]{:S(2)}) collective-permute-start(s32[96]{0:T(128)S(1)} %pad_add_fusion.1), channel_id=1, source_target_pairs={{0,1},{1,0},{2,3},{3,2},{4,5},{5,4},{6,7},{7,6},{8,9},{9,8},{10,11... | collective-permute-start | bytes 1160 | tf_op jit(solution)/shard_map/ppermute | solution.py:204
  14.2 24.3 %collective-permute-start.4 = (bf16[24,400,128]{2,1,0:T(8,128)(2,1)S(1)}, bf16[24,400,128]{2,1,0:T(8,128)(2,1)}, u32[]{:S(2)}, u32[]{:S(2)}) collective-permute-start(bf16[24,400,128]{2,1,0:T(8,128)(2,1)S(1)} %bitcast.38), channel_id=1, source_target_pairs={{0,1},{1,0},{2,3},{3,2},{4,5},{5,4},{6,7},{7,6},{8,9},{9,8},{10,11... | collective-permute-start | bytes 7372808 | tf_op jit(solution)/shard_map/ppermute | solution.py:204
  16.2 5.0 %collective-permute-start.6 = (s32[24]{0:T(128)S(1)}, s32[24]{0:T(128)S(1)}, u32[]{:S(2)}, u32[]{:S(2)}) collective-permute-start(s32[24]{0:T(128)S(1)} %reshape.489.table), channel_id=1, source_target_pairs={{0,2},{1,3},{2,0},{3,1},{4,6},{5,7},{6,4},{7,5},{8,10},{9,11},{10,... | collective-permute-start | bytes 296 | tf_op jit(solution)/shard_map/ppermute | solution.py:204
  19.4 15.3 %collective-permute-start = (f32[1624]{0:T(1024)S(1)}, f32[1624]{0:T(1024)S(1)}, u32[]{:S(2)}, u32[]{:S(2)}) collective-permute-start(f32[1624]{0:T(1024)S(1)} %get-tuple-element.54), channel_id=1, source_target_pairs={{0,4},{4,0},{8,12},{12,8},{1,5},{5,1},{9,13},{13,9},{2,6},{6,2},{1... | collective-permute-start | bytes 19496 | tf_op jit(solution)/shard_map/ppermute | solution.py:204
  21.1 13.9 %collective-permute-start.1 = (f32[1624]{0:T(1024)S(1)}, f32[1624]{0:T(1024)S(1)}, u32[]{:S(2)}, u32[]{:S(2)}) collective-permute-start(f32[1624]{0:T(1024)S(1)} %get-tuple-element.55), channel_id=1, source_target_pairs={{0,8},{4,12},{8,0},{12,4},{1,9},{5,13},{9,1},{13,5},{2,10},{6,14},... | collective-permute-start | bytes 19496 | tf_op jit(solution)/shard_map/ppermute | solution.py:204
  23.8 14.5 %collective-permute-start.2 = (f32[1624]{0:T(1024)S(1)}, f32[1624]{0:T(1024)S(1)}, u32[]{:S(2)}, u32[]{:S(2)}) collective-permute-start(f32[1624]{0:T(1024)S(1)} %get-tuple-element.56), channel_id=1, source_target_pairs={{0,12},{4,8},{8,4},{12,0},{1,13},{5,9},{9,5},{13,1},{2,14},{6,10},... | collective-permute-start | bytes 19496 | tf_op jit(solution)/shard_map/ppermute | solution.py:204
  33.5 26.9 %copy-start.8 = (bf16[6,400,128]{2,1,0:T(8,128)(2,1)}, bf16[6,400,128]{2,1,0:T(8,128)(2,1)S(1)}, u32[]{:S(2)}) copy-start(bf16[6,400,128]{2,1,0:T(8,128)(2,1)S(1)} %get-tuple-element.39) | copy-start | bytes 1843204
  34.7 77.1 %collective-permute-start.19 = (bf16[6,400,128]{2,1,0:T(8,128)(2,1)}, bf16[6,400,128]{2,1,0:T(8,128)(2,1)}, u32[]{:S(2)}, u32[]{:S(2)}) collective-permute-start(bf16[6,400,128]{2,1,0:T(8,128)(2,1)} %copy-done.10), channel_id=1, source_target_pairs={{0,4},{4,0},{8,12},{12,8},{1,5},{5,1},{9,13},{13,9},{2,6},{6,2},{1... | collective-permute-start | bytes 1843208 | tf_op jit(solution)/shard_map/ppermute | solution.py:204
  35.0 80.7 %collective-permute-start.20 = (bf16[6,400,128]{2,1,0:T(8,128)(2,1)}, bf16[6,400,128]{2,1,0:T(8,128)(2,1)}, u32[]{:S(2)}, u32[]{:S(2)}) collective-permute-start(bf16[6,400,128]{2,1,0:T(8,128)(2,1)} %copy-done.9), channel_id=1, source_target_pairs={{0,8},{4,12},{8,0},{12,4},{1,9},{5,13},{9,1},{13,5},{2,10},{6,14},... | collective-permute-start | bytes 1843208 | tf_op jit(solution)/shard_map/ppermute | solution.py:204
  40.2 41.5 %copy-start.2 = (bf16[6,128,2,1,6,128]{5,1,0,4,2,3:T(8,128)(2,1)S(1)}, bf16[6,128,2,1,6,128]{5,1,0,4,2,3:T(8,128)(2,1)}, u32[]{:S(2)}) copy-start(bf16[6,128,2,1,6,128]{5,1,0,4,2,3:T(8,128)(2,1)} %copy.62) | copy-start | bytes 7077892
  40.2 41.5 %copy-start.6 = (bf16[6,128,128]{2,1,0:T(8,128)(2,1)S(1)}, bf16[6,128,128]{2,1,0:T(8,128)(2,1)}, u32[]{:S(2)}) copy-start(bf16[6,128,128]{2,1,0:T(8,128)(2,1)} %fock_vir.1) | copy-start | bytes 589828
  58.3 22.2 %collective-permute-start.15 = (s16[8,416,128]{2,1,0:T(8,128)(2,1)}, s16[8,416,128]{2,1,0:T(8,128)(2,1)}, u32[]{:S(2)}, u32[]{:S(2)}) collective-permute-start(s16[8,416,128]{2,1,0:T(8,128)(2,1)} %get-tuple-element.31), channel_id=1, source_target_pairs={{0,2},{1,3},{2,0},{3,1},{4,6},{5,7},{6,4},{7,5},{8,10},{9,11},{10,... | collective-permute-start | bytes 2555912 | tf_op jit(solution)/shard_map/ppermute | solution.py:204
  58.3 47.3 %collective-permute-start.11 = (s16[8,416,128]{2,1,0:T(8,128)(2,1)}, s16[8,416,128]{2,1,0:T(8,128)(2,1)}, u32[]{:S(2)}, u32[]{:S(2)}) collective-permute-start(s16[8,416,128]{2,1,0:T(8,128)(2,1)} %get-tuple-element.26), channel_id=1, source_target_pairs={{0,2},{1,3},{2,0},{3,1},{4,6},{5,7},{6,4},{7,5},{8,10},{9,11},{10,... | collective-permute-start | bytes 2555912 | tf_op jit(solution)/shard_map/ppermute | solution.py:204
  60.4 56.1 %collective-permute-start.7 = (s16[8,416,128]{2,1,0:T(8,128)(2,1)}, s16[8,416,128]{2,1,0:T(8,128)(2,1)S(1)}, u32[]{:S(2)}, u32[]{:S(2)}) collective-permute-start(s16[8,416,128]{2,1,0:T(8,128)(2,1)} %get-tuple-element.21), channel_id=1, source_target_pairs={{0,2},{1,3},{2,0},{3,1},{4,6},{5,7},{6,4},{7,5},{8,10},{9,11},{10,... | collective-permute-start | bytes 2555912 | tf_op jit(solution)/shard_map/ppermute | solution.py:204
  80.5 42.3 %collective-permute-start.21 = (bf16[6,400,128]{2,1,0:T(8,128)(2,1)}, bf16[6,400,128]{2,1,0:T(8,128)(2,1)}, u32[]{:S(2)}, u32[]{:S(2)}) collective-permute-start(bf16[6,400,128]{2,1,0:T(8,128)(2,1)} %copy-done.8), channel_id=1, source_target_pairs={{0,12},{4,8},{8,4},{12,0},{1,13},{5,9},{9,5},{13,1},{2,14},{6,10},... | collective-permute-start | bytes 1843208 | tf_op jit(solution)/shard_map/ppermute | solution.py:204
  105.6 20.8 %collective-permute-start.16 = (s16[2,416,128]{2,1,0:T(8,128)(2,1)S(1)}, s16[2,416,128]{2,1,0:T(8,128)(2,1)S(1)}, u32[]{:S(2)}, u32[]{:S(2)}) collective-permute-start(s16[2,416,128]{2,1,0:T(8,128)(2,1)S(1)} %get-tuple-element.33), channel_id=1, source_target_pairs={{0,4},{4,0},{8,12},{12,8},{1,5},{5,1},{9,13},{13,9},{2,6},{6,2},{1... | collective-permute-start | bytes 638984 | tf_op jit(solution)/shard_map/ppermute | solution.py:204
  111.8 26.4 %collective-permute-start.17 = (s16[2,416,128]{2,1,0:T(8,128)(2,1)S(1)}, s16[2,416,128]{2,1,0:T(8,128)(2,1)S(1)}, u32[]{:S(2)}, u32[]{:S(2)}) collective-permute-start(s16[2,416,128]{2,1,0:T(8,128)(2,1)S(1)} %get-tuple-element.34), channel_id=1, source_target_pairs={{0,8},{4,12},{8,0},{12,4},{1,9},{5,13},{9,1},{13,5},{2,10},{6,14},... | collective-permute-start | bytes 638984 | tf_op jit(solution)/shard_map/ppermute | solution.py:204
  115.8 24.8 %collective-permute-start.18 = (s16[2,416,128]{2,1,0:T(8,128)(2,1)S(1)}, s16[2,416,128]{2,1,0:T(8,128)(2,1)S(1)}, u32[]{:S(2)}, u32[]{:S(2)}) collective-permute-start(s16[2,416,128]{2,1,0:T(8,128)(2,1)S(1)} %get-tuple-element.35), channel_id=1, source_target_pairs={{0,12},{4,8},{8,4},{12,0},{1,13},{5,9},{9,5},{13,1},{2,14},{6,10},... | collective-permute-start | bytes 638984 | tf_op jit(solution)/shard_map/ppermute | solution.py:204
  116.5 26.9 %collective-permute-start.12 = (s16[2,416,128]{2,1,0:T(8,128)(2,1)S(1)}, s16[2,416,128]{2,1,0:T(8,128)(2,1)S(1)}, u32[]{:S(2)}, u32[]{:S(2)}) collective-permute-start(s16[2,416,128]{2,1,0:T(8,128)(2,1)S(1)} %get-tuple-element.28), channel_id=1, source_target_pairs={{0,4},{4,0},{8,12},{12,8},{1,5},{5,1},{9,13},{13,9},{2,6},{6,2},{1... | collective-permute-start | bytes 638984 | tf_op jit(solution)/shard_map/ppermute | solution.py:204
  116.5 49.7 %copy-start.5 = (bf16[6,400,128]{2,1,0:T(8,128)(2,1)S(1)}, bf16[6,400,128]{2,1,0:T(8,128)(2,1)}, u32[]{:S(2)}) copy-start(bf16[6,400,128]{2,1,0:T(8,128)(2,1)} %copy-done.4) | copy-start | bytes 1843204
  116.5 49.7 %copy-start.7 = (f32[6,128]{1,0:T(8,128)S(1)}, f32[6,128]{1,0:T(8,128)}, u32[]{:S(2)}) copy-start(f32[6,128]{1,0:T(8,128)} %vir_energy.1) | copy-start | bytes 9220
  122.8 28.6 %collective-permute-start.13 = (s16[2,416,128]{2,1,0:T(8,128)(2,1)}, s16[2,416,128]{2,1,0:T(8,128)(2,1)S(1)}, u32[]{:S(2)}, u32[]{:S(2)}) collective-permute-start(s16[2,416,128]{2,1,0:T(8,128)(2,1)} %get-tuple-element.29), channel_id=1, source_target_pairs={{0,8},{4,12},{8,0},{12,4},{1,9},{5,13},{9,1},{13,5},{2,10},{6,14},... | collective-permute-start | bytes 638984 | tf_op jit(solution)/shard_map/ppermute | solution.py:204
  126.4 25.0 %collective-permute-start.14 = (s16[2,416,128]{2,1,0:T(8,128)(2,1)}, s16[2,416,128]{2,1,0:T(8,128)(2,1)S(1)}, u32[]{:S(2)}, u32[]{:S(2)}) collective-permute-start(s16[2,416,128]{2,1,0:T(8,128)(2,1)} %get-tuple-element.30), channel_id=1, source_target_pairs={{0,12},{4,8},{8,4},{12,0},{1,13},{5,9},{9,5},{13,1},{2,14},{6,10},... | collective-permute-start | bytes 638984 | tf_op jit(solution)/shard_map/ppermute | solution.py:204
  138.2 13.1 %collective-permute-start.10 = (s16[2,416,128]{2,1,0:T(8,128)(2,1)}, s16[2,416,128]{2,1,0:T(8,128)(2,1)S(1)}, u32[]{:S(2)}, u32[]{:S(2)}) collective-permute-start(s16[2,416,128]{2,1,0:T(8,128)(2,1)} %get-tuple-element.25), channel_id=1, source_target_pairs={{0,12},{4,8},{8,4},{12,0},{1,13},{5,9},{9,5},{13,1},{2,14},{6,10},... | collective-permute-start | bytes 638984 | tf_op jit(solution)/shard_map/ppermute | solution.py:204
  140.6 11.0 %collective-permute-start.8 = (s16[2,416,128]{2,1,0:T(8,128)(2,1)}, s16[2,416,128]{2,1,0:T(8,128)(2,1)S(1)}, u32[]{:S(2)}, u32[]{:S(2)}) collective-permute-start(s16[2,416,128]{2,1,0:T(8,128)(2,1)} %get-tuple-element.23), channel_id=1, source_target_pairs={{0,4},{4,0},{8,12},{12,8},{1,5},{5,1},{9,13},{13,9},{2,6},{6,2},{1... | collective-permute-start | bytes 638984 | tf_op jit(solution)/shard_map/ppermute | solution.py:204
  143.4 22.8 %collective-permute-start.9 = (s16[2,416,128]{2,1,0:T(8,128)(2,1)}, s16[2,416,128]{2,1,0:T(8,128)(2,1)S(1)}, u32[]{:S(2)}, u32[]{:S(2)}) collective-permute-start(s16[2,416,128]{2,1,0:T(8,128)(2,1)} %get-tuple-element.24), channel_id=1, source_target_pairs={{0,8},{4,12},{8,0},{12,4},{1,9},{5,13},{9,1},{13,5},{2,10},{6,14},... | collective-permute-start | bytes 638984 | tf_op jit(solution)/shard_map/ppermute | solution.py:204
  (6 other events, 8.0 us)
